TPU v7x, 256 devices: a whole 4x4x8 slice. The times are simulated.
256 devices in a mesh: row: 8 (over y, x_lo), col: 32 (over x_hi, z, core).
Axes of the slice: x: 4 (x_hi: 2, x_lo: 2; x = x_hi * 2 + x_lo), y: 4, z: 8, core: 2. Of those that a mesh axis runs over, the one named last changes fastest.
Arguments:
- inputs: bfloat16 [1024, 6144], P('col', 'row'), may hold values from -6 to 6
- gain: float32 [6144], P('row'), may hold values from 0.5 to 2
- w_in: bfloat16 [6144, 24576], P('row', 'col'), may hold values from -0.078125 to 0.078125
- bias: float32 [24576], P('col'), may hold values from -3 to 3
- w_out: bfloat16 [24576, 6144], P('col', 'row'), may hold values from -0.078125 to 0.078125
- cotangent: bfloat16 [1024, 6144], P('col', 'row'), may hold values from -6 to 6
Outputs:
- grad_input: bfloat16 [1024, 6144], P('col', 'row')
- grad_w_in: bfloat16 [6144, 24576], P('row', 'col')
- grad_bias: float32 [24576], P('col')
- grad_w_out: bfloat16 [24576, 6144], P('col', 'row')
All inputs are finite; a program needn't handle non-finite values.
Results may differ from a plain program's by a relative error of at most 0.023.
Values may be sent and summed in bfloat16 or wider, within the bound.
A program may use at most 64 MiB of HBM per device.

v0:
```python
import functools

import jax
import jax.numpy as jnp
from jax import lax
from jax.experimental import pallas as pl
from jax.experimental.pallas import tpu as pltpu
from jax.sharding import PartitionSpec as P

MESH = pl.DeviceIdType.MESH
F32, BF16 = jnp.float32, jnp.bfloat16
D = 6144
EPS = 1e-06
TOKENS, BLK = 1024, 768
CA = 256
CB = BLK - CA
HA, HB = CA // 2, CB // 2
COLS_A, COLS_B = pl.ds(0, CA), pl.ds(CA, CB)
DELTA = (0, 1, -1, 2, -2, 3, -3, 4)
CHUNKS = ((0, 1), (1, 3), (3, 5), (5, 7), (7, 8))
N_SEND, N_RECV = 40, 200


def normal_parts(pre_act):
    cumulative = 0.5 * (1.0 + lax.erf(pre_act * 0.7071067811865476))
    density = jnp.exp(-0.5 * pre_act * pre_act) * 0.3989422804014327
    return cumulative, density


def slot_of(delta):
    return DELTA.index(4 if delta in (4, -4) else delta)


def kernel(
    inp_hbm, gain_hbm, w_in_hbm, bias_hbm, w_out_hbm, cot_hbm, gi, gwi, gb, gwo,
    inp, gain, w_in, bias, w_out, gath, part, ra1, sa, raf, ra3, rbf, rb, sb, rbx, hid,
    gk, gs, gr, xs, xr, zs, zr, acc, st, ft, load_sem, send_sem, recv_sem,
):
    row, col = lax.axis_index("row"), lax.axis_index("col")
    y, xl = row // 2, row % 2
    xh, z, k = col // 16, (col // 2) % 8, col % 2

    def dev(dy=0, dx=0, dh=0, dz=0, dk=0):
        return (
            ((y + dy + 4) % 4) * 2 + (xl + dx) % 2,
            ((xh + dh) % 2) * 16 + ((z + dz + 8) % 8) * 2 + (k + dk) % 2,
        )

    xp, yp, ym, y2 = 1 - xl, (y + 1) % 4, (y + 3) % 4, (y + 2) % 4
    ROW_PEERS = [(dy, dx) for dy in range(4) for dx in range(2) if dy or dx]
    partners = [dev(dy=a, dx=b) for a, b in ROW_PEERS]
    partners += [dev(dz=1), dev(dz=-1), dev(dk=1), dev(dh=1), dev(dh=1, dk=1)]
    barrier = pltpu.get_barrier_semaphore()
    for partner in partners:
        pl.semaphore_signal(barrier, inc=1, device_id=partner, device_id_type=MESH)
    loads = [
        pltpu.make_async_copy(src, dst, load_sem.at[i])
        for i, (src, dst) in enumerate((
            (cot_hbm, gath.at[0, 0, 0, pl.ds(0, 32)]),
            (inp_hbm, inp),
            (gain_hbm, gain.at[0]),
            (bias_hbm, bias.at[0]),
            (w_out_hbm, w_out),
            (w_in_hbm, w_in),
        ))
    ]
    for load in loads:
        load.start()

    send_index, recv_index = {}, {}

    def send(key, kind, src, dst, to):
        pltpu.make_async_remote_copy(
            src_ref=src, dst_ref=dst,
            send_sem=send_sem.at[send_index.setdefault(kind, len(send_index))],
            recv_sem=recv_sem.at[recv_index.setdefault(key, len(recv_index))],
            device_id=to, device_id_type=MESH,
        ).start()

    def all_of(ref, kind, key):
        return pltpu.make_async_remote_copy(
            src_ref=ref, dst_ref=ref, send_sem=send_sem.at[send_index[kind]],
            recv_sem=recv_sem.at[recv_index[key]], device_id=dev(dk=1), device_id_type=MESH,
        )

    def arrived(key, ref):
        all_of(ref, ("st",), key).wait_recv()

    def departed(kind, ref):
        all_of(ref, kind, ("st",)).wait_send()

    lane = lax.broadcasted_iota(jnp.int32, (32, 128), 1)

    def pair(a, b):
        return jnp.where(lane < 64, a, b)

    loads[0].wait()
    loads[1].wait()
    values = inp[...].astype(F32)
    st[0] = pair(
        jnp.sum(values, 1, keepdims=True), jnp.sum(values * values, 1, keepdims=True)
    )
    pl.semaphore_wait(barrier, len(partners))

    def all_row(tag, ref):
        for i, (dy, dx) in enumerate(ROW_PEERS):
            send((tag,), (tag,), ref.at[0], ref.at[i + 1], dev(dy=dy, dx=dx))

    def row_sum(tag, ref):
        arrived((tag,), ref.at[pl.ds(1, 7)])
        total = ref[0]
        for i in range(1, 8):
            total = total + ref[i]
        return total[:, 0:1] * (1.0 / D), total[:, 64:65] * (1.0 / D)

    def unit(a, slot, u):
        return gath.at[a, slot, 0, pl.ds(u * 32, 32)]

    def pass_z(a, u, origin, slot, dz):
        send(("z", a, u, slot), ("z", a), unit(a, origin, u), unit(a, slot, u), dev(dz=dz))

    def z_first(a, u):
        pass_z(a, u, 0, 2, 1)
        pass_z(a, u, 0, 1, -1)

    def to_sibling(a, c, slot, u):
        mine = unit(a, slot, u)
        send(("k", a, c), ("k", a), mine, gath.at[a, slot, 1, pl.ds(u * 32, 32)], dev(dk=1))

    def own(a):
        mine = unit(a, 0, 0)
        send(("h", a), ("o", a), mine, unit(a, 0, 1), dev(dh=1))
        z_first(a, 0)
        send(("k", a, 0), ("o", a), mine, gath.at[a, 0, 1, pl.ds(32, 32)], dev(dh=1, dk=1))
        send(("k", a, 0), ("o", a), mine, gath.at[a, 0, 1, pl.ds(0, 32)], dev(dk=1))

    def other(a):
        arrived(("h", a), unit(a, 0, 1))
        z_first(a, 1)

    def hop(a, u, h):
        if h == 4:
            arrived(("z", a, u, 7), unit(a, 7, u))
            to_sibling(a, h, 7, u)
            return
        for slot, dz in ((slot_of(-h), 1), (slot_of(h), -1)):
            arrived(("z", a, u, slot), unit(a, slot, u))
            if h < 3 or u == (dz < 0):
                pass_z(a, u, slot, slot_of(-dz * (h + 1)), dz)
            to_sibling(a, h, slot, u)

    def span(c):
        s0, s1 = CHUNKS[c]
        return s0 * 128, (s1 - s0) * 128

    def at(base, index, size):
        return pl.ds(pl.multiple_of(base + index * size, 16), size)

    def product(a, c):
        off, t = span(c)
        s0, s1 = CHUNKS[c]
        arrived(("k", a, c), gath.at[a, pl.ds(s0, s1 - s0), 1])
        rows = gath[a, s0:s1].reshape(t, BLK)
        if a == 0:
            out = lax.dot_general(
                rows, w_out[...], (((1,), (1,)), ((), ())), preferred_element_type=F32
            )
        else:
            out = jnp.dot(rows, w_in[...], preferred_element_type=F32)
        part[a, off:off + t, :] = out.astype(BF16)
        far = at(off, y2, t // 4)
        quarter = pl.ds(off // 4, t // 4)
        for i, dy in ((0, 1), (1, -1)):
            send(
                ("bf", a, c), ("p", a), part.at[a, far, pl.ds(CA + i * HB, HB)],
                rbf.at[a, i, quarter], dev(dy=dy),
            )
        send(
            ("a1", a, c), ("p", a), part.at[a, at(off, xp, t // 2), COLS_A],
            ra1.at[a, pl.ds(off // 2, t // 2)], dev(dx=1),
        )

    def merge(ref, a, rows, cols, other):
        ref[a, rows, cols] = (ref[a, rows, cols].astype(F32) + other.astype(F32)).astype(BF16)

    def reduce2(a, c):
        off, t = span(c)
        o2, o4, o8, t2, t4, t8 = off // 2, off // 4, off // 8, t // 2, t // 4, t // 8
        arrived(("bf", a, c), rbf.at[a, :, pl.ds(o4, t4)])
        for i, block, start, dy in ((0, yp, CA, 1), (1, ym, CA + HB, -1)):
            merge(part, a, at(off, block, t4), pl.ds(start, HB), rbf[a, i, o4:o4 + t4])
            send(
                ("b", a, c), ("b", a), part.at[a, at(off, block, t4), COLS_B],
                rb.at[a, i, pl.ds(o4, t4)], dev(dy=dy),
            )
        arrived(("a1", a, c), ra1.at[a, pl.ds(o2, t2)])
        total = part[a, at(off, xl, t2), COLS_A].astype(F32) + ra1[a, o2:o2 + t2].astype(F32)
        sa[a, o2:o2 + t2] = total.astype(BF16)
        for i, dy in ((0, 1), (1, -1)):
            send(
                ("af", a, c), ("af", a), sa.at[a, at(o2, y2, t8), pl.ds(i * HA, HA)],
                raf.at[a, i, pl.ds(o8, t8)], dev(dy=dy),
            )

    def reduce3(a, c):
        off, t = span(c)
        o2, o4, o8, t4, t8 = off // 2, off // 4, off // 8, t // 4, t // 8
        arrived(("af", a, c), raf.at[a, :, pl.ds(o8, t8)])
        for i, block, start, dy in ((0, yp, 0, 1), (1, ym, HA, -1)):
            merge(sa, a, at(o2, block, t8), pl.ds(start, HA), raf[a, i, o8:o8 + t8])
            send(
                ("a3", a, c), ("a3", a), sa.at[a, at(o2, block, t8)],
                ra3.at[a, i, pl.ds(o8, t8)], dev(dy=dy),
            )
        arrived(("b", a, c), rb.at[a, :, pl.ds(o4, t4)])
        total = part[a, at(off, y, t4), COLS_B].astype(F32)
        for i in (0, 1):
            total = total + rb[a, i, o4:o4 + t4].astype(F32)
        sb[a, o4:o4 + t4] = total.astype(BF16)
        send(
            ("b3", a, c), ("b3", a), sb.at[a, at(o4, xp, t8)], rbx.at[a, pl.ds(o8, t8)],
            dev(dx=1),
        )

    def rows_a(c):
        off, t = span(c)
        return at(off, xl * 4 + y, t // 8)

    def rows_b(c):
        off, t = span(c)
        return at(off, y * 2 + xl, t // 8)

    def elementwise(c):
        off, t = span(c)
        o2, o4, o8, t8 = off // 2, off // 4, off // 8, t // 8

        def finish(rows, cols, bias_part, totals):
            pre_act = totals[1] + bias_part
            cumulative, density = normal_parts(pre_act)
            hid[0, rows, cols] = (totals[0] * (cumulative + pre_act * density)).astype(BF16)
            hid[1, rows, cols] = (pre_act * cumulative).astype(BF16)

        totals = []
        for a in (0, 1):
            arrived(("a3", a, c), ra3.at[a, :, pl.ds(o8, t8)])
            total = sa[a, at(o2, y, t8)].astype(F32)
            for i in (0, 1):
                total = total + ra3[a, i, o8:o8 + t8].astype(F32)
            totals.append(total)
        finish(rows_a(c), COLS_A, bias[:, 0:CA], totals)
        totals = []
        for a in (0, 1):
            arrived(("b3", a, c), rbx.at[a, pl.ds(o8, t8)])
            totals.append(sb[a, at(o4, xl, t8)].astype(F32) + rbx[a, o8:o8 + t8].astype(F32))
        finish(rows_b(c), COLS_B, bias[:, CA:BLK], totals)

    def share(key, kind, ref, to):
        send(key, kind, ref, ref, to)

    def block_a(g, c, index, cols=COLS_A):
        off, t = span(c)
        return hid.at[g, at(off, xl * 4 + index, t // 8), cols]

    def block_b(g, c, index, cols=COLS_B):
        off, t = span(c)
        return hid.at[g, at(off, index, t // 4), cols]

    def gather1(g, c):
        share(("h1", g, c), ("g1", g), hid.at[g, rows_b(c), COLS_B], dev(dx=1))
        for i, dy in ((0, 1), (1, -1)):
            share(("g1", g, c, i), ("g1", g), block_a(g, c, y), dev(dy=dy))

    def gather2(g, c):
        off, t = span(c)
        arrived(("h1", g, c), hid.at[g, at(off, y * 2 + xp, t // 8), COLS_B])
        for i, dy in ((0, 1), (1, -1)):
            share(("h2", g, c, i), ("h2", g), block_b(g, c, y), dev(dy=dy))
        for i, block, dy in ((0, ym, 1), (1, yp, -1)):
            arrived(("g1", g, c, i), block_a(g, c, block))
            share(("g2", g, c), ("g2", g), block_a(g, c, block, pl.ds(i * HA, HA)), dev(dy=dy))

    def gather3(g, c):
        off, t = span(c)
        for i, block, dy in ((0, ym, 1), (1, yp, -1)):
            arrived(("h2", g, c, i), block_b(g, c, block))
            share(("h3", g, c), ("g3", g), block_b(g, c, block, pl.ds(CA + i * HB, HB)), dev(dy=dy))
        arrived(("g2", g, c), block_a(g, c, y2))
        share(("g3", g, c), ("g3", g), hid.at[g, at(off, xl, t // 2), COLS_A], dev(dx=1))

    def gathered(g, c):
        off, t = span(c)
        arrived(("g3", g, c), hid.at[g, at(off, xp, t // 2), COLS_A])
        arrived(("h3", g, c), block_b(g, c, y2))

    def back_product(c):
        gathered(0, c)
        off, t = span(c)
        s0, s1 = CHUNKS[c]
        out = lax.dot_general(
            hid[0, off:off + t, :], w_in[...], (((1,), (1,)), ((), ())),
            preferred_element_type=F32,
        )
        for slot in range(s0, s1):
            base = (slot - s0) * 128
            gk[slot] = out[base:base + 64]
            gs[slot] = out[base + 64:base + 128].astype(BF16)
        send(("n", c), ("n",), gs.at[pl.ds(s0, s1 - s0)], gr.at[pl.ds(s0, s1 - s0)], dev(dk=1))

    def scatter_x(c):
        s0, s1 = CHUNKS[c]
        arrived(("n", c), gr.at[pl.ds(s0, s1 - s0)])
        for slot in range(s0, s1):
            total = gk[slot] + gr[slot].astype(F32)
            gk[slot, 0:32] = total[0:32]
            xs[slot] = total[32:64].astype(BF16)
        send(("x", c), ("x",), xs.at[pl.ds(s0, s1 - s0)], xr.at[pl.ds(s0, s1 - s0)], dev(dh=1))

    def scatter_z(c):
        s0, s1 = CHUNKS[c]
        arrived(("x", c), xr.at[pl.ds(s0, s1 - s0)])
        for slot in range(s0, s1):
            total = gk[slot, 0:32] + xr[slot].astype(F32)
            if slot == 0:
                gk[0, 0:32] = total
            else:
                zs[slot] = total.astype(BF16)
                send(("s",), ("s",), zs.at[slot], zr.at[slot], dev(dz=DELTA[slot]))

    scale = float(TOKENS) ** (-0.5)
    tiles = [(i * 256, (i + 1) * 256) for i in range(3)]

    def outer(left, right):
        return lax.dot_general(
            left, right, (((0,), (0,)), ((), ())), preferred_element_type=F32
        )

    def flat(a, s0=0, s1=8):
        return gath[a, s0:s1].reshape((s1 - s0) * 128, BLK)

    def grad_in():
        for i, j in tiles:
            gwi[i:j, :] = (outer(flat(1)[:, i:j], hid[0]) * scale).astype(BF16)
        gb[...] = (jnp.sum(hid[0].astype(F32), 0, keepdims=True) * scale).reshape(BLK)

    def total_back():
        total = gk[0, 0:32]
        arrived(("s",), zr.at[pl.ds(1, 7)])
        for slot in range(1, 8):
            total = total + zr[slot].astype(F32)
        scaled = total * gain[...]
        ft[0] = pair(
            jnp.sum(scaled, 1, keepdims=True), jnp.sum(scaled * centred, 1, keepdims=True)
        )
        all_row("ft", ft)
        return scaled

    def finish_input(scaled):
        first, cross = row_sum("ft", ft)
        gi[...] = (inv_std * (scaled - first - centred * cross)).astype(BF16)

    def partial_out():
        for c in range(4):
            gathered(1, c)
        for i, j in tiles:
            acc[i:j, :] = outer(hid[1, 0:896, i:j], flat(0, 0, 7))

    def last_out():
        gathered(1, 4)
        for i, j in tiles:
            gwo[i:j, :] = (
                (acc[i:j, :] + outer(hid[1, 896:TOKENS, i:j], flat(0, 7, 8))) * scale
            ).astype(BF16)

    own(0)
    all_row("st", st)
    mean_x, second = row_sum("st", st)
    inv_std = lax.rsqrt(second - mean_x * mean_x + EPS)
    centred = (values - mean_x) * inv_std
    loads[2].wait()
    gath[1, 0, 0, 0:32] = (centred * gain[...]).astype(BF16)
    own(1)
    other(0)
    hop(0, 0, 1)
    loads[4].wait()
    product(0, 0)
    other(1)
    loads[5].wait()
    product(1, 0)
    hop(0, 1, 1)
    hop(1, 0, 1)
    reduce2(0, 0)
    product(0, 1)
    hop(1, 1, 1)
    hop(0, 0, 2)
    reduce2(1, 0)
    hop(0, 1, 2)
    product(1, 1)
    reduce3(0, 0)
    product(0, 2)
    hop(1, 0, 2)
    reduce2(0, 1)
    hop(1, 1, 2)
    reduce3(1, 0)
    hop(0, 0, 3)
    product(1, 2)
    reduce2(1, 1)
    hop(0, 1, 3)
    reduce2(0, 2)
    reduce3(0, 1)
    product(0, 3)
    hop(1, 1, 3)
    hop(1, 0, 3)
    hop(0, 0, 4)
    reduce2(1, 2)
    hop(0, 1, 4)
    product(1, 3)
    reduce3(1, 1)
    hop(1, 1, 4)
    hop(1, 0, 4)
    product(0, 4)
    reduce2(0, 3)
    product(1, 4)
    reduce3(1, 2)
    reduce3(0, 2)
    loads[3].wait()
    elementwise(0)
    reduce2(0, 4)
    elementwise(1)
    gather1(0, 1)
    reduce2(1, 3)
    elementwise(2)
    gather1(0, 2)
    reduce2(1, 4)
    gather2(0, 1)
    gather1(0, 0)
    reduce3(1, 3)
    reduce3(0, 3)
    reduce3(1, 4)
    reduce3(0, 4)
    gather2(0, 2)
    gather3(0, 1)
    elementwise(3)
    gather1(0, 3)
    elementwise(4)
    gather2(0, 0)
    gather1(0, 4)
    gather1(1, 0)
    gather1(1, 2)
    gather3(0, 2)
    gather2(0, 3)
    gather2(0, 4)
    gather3(0, 0)
    gather1(1, 3)
    gather1(1, 1)
    back_product(1)
    gather1(1, 4)
    back_product(2)
    gather3(0, 3)
    gather3(0, 4)
    scatter_x(1)
    back_product(0)
    gather2(1, 2)
    scatter_x(2)
    gather2(1, 0)
    gather2(1, 3)
    scatter_x(0)
    gather2(1, 4)
    back_product(4)
    back_product(3)
    scatter_x(4)
    scatter_z(1)
    gather2(1, 1)
    scatter_z(2)
    scatter_x(3)
    gather3(1, 0)
    gather3(1, 2)
    scatter_z(4)
    scatter_z(3)
    scatter_z(0)
    gather3(1, 3)
    gather3(1, 1)
    gather3(1, 4)
    grad_in()
    scaled = total_back()
    partial_out()
    last_out()
    finish_input(scaled)

    for a in (0, 1):
        departed(("z", a), gath.at[a, pl.ds(0, 7), 0])
        departed(("k", a), gath.at[a, pl.ds(0, 7), 0])
        departed(("o", a), w_in.at[pl.ds(0, 96)])
        departed(("p", a), part.at[a, :, pl.ds(0, 256)])
        departed(("b", a), part.at[a, :, pl.ds(0, 256)])
        departed(("af", a), sa.at[a, pl.ds(0, 128)])
        departed(("a3", a), rbx.at[a])
        departed(("b3", a), rbx.at[a])
        departed(("g1", a), sb.at[a])
        departed(("h2", a), hid.at[a, :, pl.ds(0, 256)])
        departed(("g2", a), sa.at[a, pl.ds(0, 128)])
        departed(("g3", a), hid.at[a, :, pl.ds(0, 256)])
    departed(("n",), gs)
    departed(("x",), xs)
    departed(("s",), zs.at[pl.ds(1, 7)])
    departed(("st",), st.at[pl.ds(1, 7)])
    departed(("ft",), ft.at[pl.ds(1, 7)])


def deliver(*refs):
    for source, target in zip(refs[:4], refs[4:]):
        target[...] = source[...]


def local(inputs, gain, w_in, bias, w_out, cotangent):
    vmem = pl.BlockSpec(memory_space=pltpu.VMEM)
    anywhere = pl.BlockSpec(memory_space=pl.ANY)
    shapes = (
        jax.ShapeDtypeStruct((32, BLK), BF16),
        jax.ShapeDtypeStruct((BLK, BLK), BF16),
        jax.ShapeDtypeStruct((BLK,), F32),
        jax.ShapeDtypeStruct((BLK, BLK), BF16),
    )
    results = pl.pallas_call(
        kernel,
        out_shape=shapes,
        in_specs=[anywhere] * 6,
        out_specs=[vmem] * 4,
        scratch_shapes=[
            pltpu.VMEM((32, BLK), BF16),
            pltpu.VMEM((1, BLK), F32),
            pltpu.VMEM((BLK, BLK), BF16),
            pltpu.VMEM((1, BLK), F32),
            pltpu.VMEM((BLK, BLK), BF16),
            pltpu.VMEM((2, 8, 2, 64, BLK), BF16),
            pltpu.VMEM((2, TOKENS, BLK), BF16),
            pltpu.VMEM((2, TOKENS // 2, CA), BF16),
            pltpu.VMEM((2, TOKENS // 2, CA), BF16),
            pltpu.VMEM((2, 2, TOKENS // 8, HA), BF16),
            pltpu.VMEM((2, 2, TOKENS // 8, CA), BF16),
            pltpu.VMEM((2, 2, TOKENS // 4, HB), BF16),
            pltpu.VMEM((2, 2, TOKENS // 4, CB), BF16),
            pltpu.VMEM((2, TOKENS // 4, CB), BF16),
            pltpu.VMEM((2, TOKENS // 8, CB), BF16),
            pltpu.VMEM((2, TOKENS, BLK), BF16),
            pltpu.VMEM((8, 64, BLK), F32),
            pltpu.VMEM((8, 64, BLK), BF16),
            pltpu.VMEM((8, 64, BLK), BF16),
            pltpu.VMEM((8, 32, BLK), BF16),
            pltpu.VMEM((8, 32, BLK), BF16),
            pltpu.VMEM((8, 32, BLK), BF16),
            pltpu.VMEM((8, 32, BLK), BF16),
            pltpu.VMEM((BLK, BLK), F32),
            pltpu.VMEM((8, 32, 128), F32),
            pltpu.VMEM((8, 32, 128), F32),
            pltpu.SemaphoreType.DMA((6,)),
            pltpu.SemaphoreType.DMA((N_SEND,)),
            pltpu.SemaphoreType.DMA((N_RECV,)),
        ],
        compiler_params=pltpu.CompilerParams(
            collective_id=0, has_side_effects=True, vmem_limit_bytes=56 * 2**20
        ),
        name="mlp_backward",
    )(inputs, gain, w_in, bias, w_out, cotangent)
    return pl.pallas_call(
        deliver,
        out_shape=shapes,
        in_specs=[vmem] * 4,
        out_specs=[vmem] * 4,
        name="deliver",
    )(*results)


def solution(mesh):
    in_specs = (
        P("col", "row"),
        P("row"),
        P("row", "col"),
        P("col"),
        P("col", "row"),
        P("col", "row"),
    )
    out_specs = (P("col", "row"), P("row", "col"), P("col"), P("col", "row"))
    return jax.shard_map(local, mesh=mesh, in_specs=in_specs, out_specs=out_specs, check_vma=False)
```

profile of v0, /device:TPU:1, one launch (start us, length us, event | category | flops | bytes accessed | tf_op | source)
XLA Modules:
  0.0 88.0 jit_solution(13019433235693704200)
XLA Ops:
  0.6 84.3 %mlp_backward.1 = (bf16[32,768]{1,0:T(8,128)(2,1)}, bf16[768,768]{1,0:T(8,128)(2,1)}, f32[768]{0:T(1024)}, bf16[768,768]{1,0:T(8,128)(2,1)}) custom-call(bf16[32,768]{1,0:T(8,128)(2,1)} %inp_hbm.1, f32[768]{0:T(1024)} %gain_hbm.1, bf16[768,768]{1,0:T(8,128)(2,1)} %w_in_hbm.1, f32[768]{0:T(1024)} %bias_hbm.1, bf16[768,768]{1,0:T(8,128)(2,1)} %w_out_hbm.1, ...), custom_call_target="tpu_custom_call" | custom-call | tf_op jit(solution)/shard_map/mlp_backward/pallas_call | solution.py:523
  84.9 3.1 %deliver.1 = (bf16[32,768]{1,0:T(8,128)(2,1)}, bf16[768,768]{1,0:T(8,128)(2,1)}, f32[768]{0:T(1024)}, bf16[768,768]{1,0:T(8,128)(2,1)}) custom-call(bf16[32,768]{1,0:T(8,128)(2,1)} %get-tuple-element.8.refs_0_, bf16[768,768]{1,0:T(8,128)(2,1)} %get-tuple-element.9.refs_1_, f32[768]{0:T(1024)} %get-tuple-element.10.refs_2_, ...), custom_call_target="tpu_custom_call" | custom-call | tf_op jit(solution)/shard_map/deliver/pallas_call | solution.py:564
where the time goes:
time: 88.2 us; the launch traced here: 88 us
  Pallas kernels  87.4 us (99%)
    pallas_call x1, Pallas kernels, local(): pl.pallas_call(kernel, out_shape=shapes, in_specs=[anywhere] * 6, out_spe...  84.3 us
    pallas_call x1, Pallas kernels, local(): pl.pallas_call(deliver, out_shape=shapes, in_specs=[vmem] * 4, out_specs=...  3.15 us

commit v1 on v0

--- a/solution.py
+++ b/solution.py
@@ -292,8 +292,16 @@
         arrived(("g3", g, c), hid.at[g, at(off, xp, t // 2), COLS_A])
         arrived(("h3", g, c), block_b(g, c, y2))
 
+    ready = set()
+
+    def all_gathered(g, chunks):
+        for c in chunks:
+            if (g, c) not in ready:
+                ready.add((g, c))
+                gathered(g, c)
+
     def back_product(c):
-        gathered(0, c)
+        all_gathered(0, (c,))
         off, t = span(c)
         s0, s1 = CHUNKS[c]
         out = lax.dot_general(
@@ -337,10 +345,12 @@
     def flat(a, s0=0, s1=8):
         return gath[a, s0:s1].reshape((s1 - s0) * 128, BLK)
 
-    def grad_in():
-        for i, j in tiles:
-            gwi[i:j, :] = (outer(flat(1)[:, i:j], hid[0]) * scale).astype(BF16)
-        gb[...] = (jnp.sum(hid[0].astype(F32), 0, keepdims=True) * scale).reshape(BLK)
+    def grad_in(n):
+        all_gathered(0, range(5))
+        i, j = tiles[n]
+        gwi[i:j, :] = (outer(flat(1)[:, i:j], hid[0]) * scale).astype(BF16)
+        if n == 0:
+            gb[...] = (jnp.sum(hid[0].astype(F32), 0, keepdims=True) * scale).reshape(BLK)
 
     def total_back():
         total = gk[0, 0:32]
@@ -358,14 +368,15 @@
         first, cross = row_sum("ft", ft)
         gi[...] = (inv_std * (scaled - first - centred * cross)).astype(BF16)
 
-    def partial_out():
-        for c in range(4):
-            gathered(1, c)
+    def partial_out(n):
+        all_gathered(1, (2 * n, 2 * n + 1))
+        s0, s1 = CHUNKS[2 * n][0], CHUNKS[2 * n + 1][1]
         for i, j in tiles:
-            acc[i:j, :] = outer(hid[1, 0:896, i:j], flat(0, 0, 7))
+            part_sum = outer(hid[1, s0 * 128:s1 * 128, i:j], flat(0, s0, s1))
+            acc[i:j, :] = acc[i:j, :] + part_sum if n else part_sum
 
     def last_out():
-        gathered(1, 4)
+        all_gathered(1, (4,))
         for i, j in tiles:
             gwo[i:j, :] = (
                 (acc[i:j, :] + outer(hid[1, 896:TOKENS, i:j], flat(0, 7, 8))) * scale
@@ -406,83 +417,86 @@
     reduce2(1, 1)
     hop(0, 1, 3)
     reduce2(0, 2)
-    reduce3(0, 1)
-    product(0, 3)
     hop(1, 1, 3)
     hop(1, 0, 3)
-    hop(0, 0, 4)
+    product(0, 3)
+    product(1, 3)
     reduce2(1, 2)
-    hop(0, 1, 4)
-    product(1, 3)
-    reduce3(1, 1)
-    hop(1, 1, 4)
-    hop(1, 0, 4)
-    product(0, 4)
-    reduce2(0, 3)
-    product(1, 4)
-    reduce3(1, 2)
-    reduce3(0, 2)
     loads[3].wait()
     elementwise(0)
+    reduce3(1, 1)
+    hop(1, 0, 4)
+    hop(0, 0, 4)
+    reduce3(0, 1)
+    hop(0, 1, 4)
+    reduce2(0, 3)
+    product(0, 4)
+    hop(1, 1, 4)
+    product(1, 4)
+    reduce2(1, 3)
+    elementwise(1)
+    reduce3(0, 2)
+    reduce3(1, 2)
+    gather1(0, 1)
+    reduce2(1, 4)
+    reduce3(0, 3)
     reduce2(0, 4)
-    elementwise(1)
-    gather1(0, 1)
-    reduce2(1, 3)
+    reduce3(1, 3)
     elementwise(2)
     gather1(0, 2)
-    reduce2(1, 4)
     gather2(0, 1)
     gather1(0, 0)
-    reduce3(1, 3)
-    reduce3(0, 3)
+    gather1(1, 0)
     reduce3(1, 4)
     reduce3(0, 4)
-    gather2(0, 2)
-    gather3(0, 1)
     elementwise(3)
     gather1(0, 3)
+    gather2(0, 2)
+    gather1(1, 1)
+    gather3(0, 1)
     elementwise(4)
-    gather2(0, 0)
     gather1(0, 4)
-    gather1(1, 0)
-    gather1(1, 2)
+    gather2(0, 3)
     gather3(0, 2)
-    gather2(0, 3)
     gather2(0, 4)
-    gather3(0, 0)
+    back_product(1)
     gather1(1, 3)
-    gather1(1, 1)
-    back_product(1)
-    gather1(1, 4)
+    gather3(0, 3)
     back_product(2)
-    gather3(0, 3)
     gather3(0, 4)
     scatter_x(1)
-    back_product(0)
-    gather2(1, 2)
+    gather2(1, 0)
+    gather2(0, 0)
     scatter_x(2)
-    gather2(1, 0)
+    gather1(1, 4)
+    gather2(1, 1)
+    back_product(4)
     gather2(1, 3)
-    scatter_x(0)
-    gather2(1, 4)
-    back_product(4)
+    gather1(1, 2)
     back_product(3)
     scatter_x(4)
     scatter_z(1)
-    gather2(1, 1)
+    gather3(0, 0)
+    gather2(1, 4)
     scatter_z(2)
     scatter_x(3)
     gather3(1, 0)
+    scatter_z(4)
+    gather2(1, 2)
+    back_product(0)
+    gather3(1, 1)
+    grad_in(1)
+    scatter_x(0)
+    scatter_z(3)
+    gather3(1, 3)
+    grad_in(2)
     gather3(1, 2)
-    scatter_z(4)
-    scatter_z(3)
+    gather3(1, 4)
+    partial_out(0)
+    grad_in(0)
     scatter_z(0)
-    gather3(1, 3)
-    gather3(1, 1)
-    gather3(1, 4)
-    grad_in()
     scaled = total_back()
-    partial_out()
+    partial_out(1)
     last_out()
     finish_input(scaled)
 
@@ -507,8 +521,15 @@
 
 
 def deliver(*refs):
-    for source, target in zip(refs[:4], refs[4:]):
-        target[...] = source[...]
+    sources, targets, sem = refs[:4], refs[4:8], refs[8]
+    copies = [
+        pltpu.make_async_copy(src, dst, sem.at[i])
+        for i, (src, dst) in enumerate(zip(sources, targets))
+    ]
+    for copy in copies:
+        copy.start()
+    for copy in copies:
+        copy.wait()
 
 
 def local(inputs, gain, w_in, bias, w_out, cotangent):
@@ -522,7 +543,7 @@
     )
     results = pl.pallas_call(
         kernel,
-        out_shape=shapes,
+        out_shape=tuple(pltpu.VMEM(x.shape, x.dtype) for x in shapes),
         in_specs=[anywhere] * 6,
         out_specs=[vmem] * 4,
         scratch_shapes=[
@@ -565,7 +586,9 @@
         deliver,
         out_shape=shapes,
         in_specs=[vmem] * 4,
-        out_specs=[vmem] * 4,
+        out_specs=[anywhere] * 4,
+        scratch_shapes=[pltpu.SemaphoreType.DMA((4,))],
+        compiler_params=pltpu.CompilerParams(vmem_limit_bytes=4 * 2**20),
         name="deliver",
     )(*results)
 

time: 88.2 us -> 82.7 us (0.938)
  Pallas kernels: 87.4 us -> 81.7 us
    pallas_call x1, Pallas kernels: 84.3 us -> 80.3 us  [local(): pl.pallas_call(kernel, out_shape=tuple((pltpu.VMEM(x.shape, x.dtype) for...]
    pallas_call x1, Pallas kernels: 3.15 us -> 1.46 us  [local(): pl.pallas_call(deliver, out_shape=shapes, in_specs=[vmem] * 4, out_specs=...]
where the time goes in v1:
time: 82.7 us; the launch traced here: 82.4 us
  Pallas kernels  81.7 us (99%)
    pallas_call x1, Pallas kernels, local(): pl.pallas_call(kernel, out_shape=tuple((pltpu.VMEM(x.shape, x.dtype) for...  80.3 us

profile of v1, /device:TPU:1, one launch (start us, length us, event | category | flops | bytes accessed | tf_op | source)
XLA Modules:
  0.0 82.4 jit_solution(10936289624592872396)
XLA Ops:
  0.6 80.3 %mlp_backward.1 = (bf16[32,768]{1,0:T(8,128)(2,1)S(1)}, bf16[768,768]{1,0:T(8,128)(2,1)S(1)}, f32[768]{0:T(1024)S(1)}, bf16[768,768]{1,0:T(8,128)(2,1)S(1)}) custom-call(bf16[32,768]{1,0:T(8,128)(2,1)} %inp_hbm.1, f32[768]{0:T(1024)} %gain_hbm.1, bf16[768,768]{1,0:T(8,128)(2,1)} %w_in_hbm.1, f32[768]{0:T(1024)} %bias_hbm.1, bf16[768,768]{1,0:T(8,128)(2,1)} %w_out_hbm.1, ...), custom_call_target="tpu_custom_call" | custom-call | tf_op jit(solution)/shard_map/mlp_backward/pallas_call | solution.py:544
  80.9 1.5 %deliver.1 = (bf16[32,768]{1,0:T(8,128)(2,1)}, bf16[768,768]{1,0:T(8,128)(2,1)}, f32[768]{0:T(1024)}, bf16[768,768]{1,0:T(8,128)(2,1)}) custom-call(bf16[32,768]{1,0:T(8,128)(2,1)S(1)} %get-tuple-element.8.refs_0_, bf16[768,768]{1,0:T(8,128)(2,1)S(1)} %get-tuple-element.9.refs_1_, f32[768]{0:T(1024)S(1)} %get-tuple-element.10.refs_2_, ...), custom_call_target="tpu_custom_call" | custom-call | tf_op jit(solution)/shard_map/deliver/pallas_call | solution.py:585
